TPU v7x, 256 devices: a whole 4x4x8 slice. The times are simulated.
256 devices in a mesh: ev: 4 (over z_hi, core), st: 64 (over x, z_lo, y).
Axes of the slice: x: 4, y: 4, z: 8 (z_hi: 2, z_lo: 4; z = z_hi * 4 + z_lo), core: 2. Of those that a mesh axis runs over, the one named last changes fastest.
Arguments:
- waveforms: bfloat16 [192, 512, 384], P('st', 'ev'), may hold values from -160 to 160
- availability: int32 [192, 512], P('st', 'ev'), may hold values 0 or 1
- lag_offset: int32 [192], P('st'), may hold values from -4 to 4
Outputs:
- correlation: float32 [17, 512, 512], P(None, ('ev', 'st'))
All inputs are finite; a program needn't handle non-finite values. No bound on the sum of `availability` on one device may be relied on, other than what follows from the above.
Results may differ from a plain program's by a relative error of at most 0.0024.
Values may be sent and summed in bfloat16 or wider, within the bound.
A program may use at most 128 MiB of HBM per device.

v0:
```python
import jax
import jax.numpy as jnp
from jax import lax
from jax.sharding import PartitionSpec as P

LAGS = 17
SHIFT_MOST = 4


epsilon = 1e-06


def normalize(waveforms, availability):
    wave_float = waveforms.astype(jnp.float32)
    energy = jnp.sum(wave_float * wave_float, axis=-1, keepdims=True)
    inverse_norm = availability.astype(jnp.float32)[..., None] * lax.rsqrt(energy + epsilon)
    return (wave_float * inverse_norm).astype(jnp.bfloat16)


def lag_stack(other_rows, shift_now):
    rows_other = other_rows.shape[0]
    samples = other_rows.shape[1] // 3
    pad_reach = SHIFT_MOST + (LAGS - 1) // 2
    split_rows = other_rows.reshape(rows_other, 3, samples)
    padded = jnp.pad(split_rows, ((0, 0), (0, 0), (pad_reach, pad_reach)))
    window = lax.dynamic_slice_in_dim(padded, SHIFT_MOST + shift_now, samples + LAGS - 1, 2)
    shifted = jnp.stack(
        [window[:, :, lag_index : lag_index + samples] for lag_index in range(LAGS)], 0
    )
    return shifted.reshape(LAGS, rows_other, 3 * samples)


def station_terms(own_block, other_block, offsets):
    shifted = jax.vmap(lag_stack)(other_block, offsets)
    return jnp.einsum("sik,sljk->lij", own_block, shifted, preferred_element_type=jnp.float32)


def on_device(waveforms, availability, lag_offset):
    unit_waves = normalize(waveforms, availability)
    ev_count = lax.axis_size("ev")
    ev_rows = unit_waves.shape[1]
    columns = ev_rows * ev_count
    gathered = lax.all_gather(unit_waves, "ev", axis=1, tiled=True)
    blocks = [
        (gathered[:, member * ev_rows : (member + 1) * ev_rows], jnp.int32(member * ev_rows))
        for member in range(ev_count)
    ]
    totals = jnp.zeros((LAGS, ev_rows, columns), jnp.float32)
    for other_block, first_col in blocks:
        partial_value = station_terms(unit_waves, other_block, lag_offset)
        totals = lax.dynamic_update_slice(totals, partial_value, (0, 0, first_col))
    return lax.psum_scatter(totals, "st", scatter_dimension=1, tiled=True)


def solution(mesh):
    placed = (P("st", "ev", None), P("st", "ev"), P("st"))
    return jax.shard_map(
        on_device,
        mesh=mesh,
        in_specs=placed,
        out_specs=P(None, ("ev", "st"), None),
        check_vma=False,
    )
```

profile of v0, /device:TPU:0, one launch (start us, length us, event | category | flops | bytes accessed | tf_op | source)
XLA Modules:
  0.0 487.4 jit_solution(12378270814222042738)
XLA Ops:
  6.5 1.2 copy.27
  7.8 0.7 rsqrt_multiply_fusion
  8.5 0.8 fusion.4
  9.3 0.7 fusion.78
  10.0 34.0 %all-gather.2.cloned.1.call-done = bf16[3,512,384]{1,2,0:T(8,128)(2,1)} async-done(((bf16[3,128,384]{1,2,0:T(8,128)(2,1)}), bf16[3,512,384]{1,2,0:T(8,128)(2,1)}) %all-gather.2.cloned.1.call-update) | async-done | bytes 1179664 | tf_op jit(solution)/shard_map/all_gather | solution.py:43
  44.0 1.3 fusion.79
  45.3 0.3 copy.28
  45.7 1.2 gather_fusion
  47.0 0.2 fusion.71
  47.4 0.2 fusion.69
  47.6 0.2 fusion.68
  47.7 0.2 fusion.67
  47.9 0.2 fusion.66
  48.1 0.2 fusion.65
  48.3 0.2 fusion.64
  48.4 0.2 fusion.63
  49.5 0.2 fusion.57
  49.8 1.5 copy.29
  51.3 1.5 convolution_bitcast_fusion.3
  52.8 0.3 copy.32
  53.3 1.2 gather_fusion.1
  54.6 0.2 fusion.54
  54.9 0.2 fusion.52
  55.1 0.2 fusion.51
  55.3 0.2 fusion.50
  55.5 0.2 fusion.49
  55.6 0.2 fusion.48
  55.8 0.2 fusion.47
  56.0 0.2 fusion.46
  56.3 0.2 fusion.44
  56.5 0.2 fusion.43
  57.0 0.2 fusion.40
  57.4 3.7 copy.33
  61.0 0.3 copy.36
  61.5 1.3 gather_fusion.2
  63.0 0.2 fusion.37
  63.3 0.2 fusion.35
  63.5 0.2 fusion.34
  63.7 0.2 fusion.33
  63.8 0.2 fusion.32
  64.0 0.2 fusion.31
  64.2 0.2 fusion.30
  64.4 0.2 fusion.29
  65.4 0.2 fusion.23
  65.7 3.8 copy.37
  69.5 0.3 copy.40
  69.9 1.2 gather_fusion.3
  71.2 0.2 fusion.20
  71.6 0.2 fusion.18
  71.8 0.2 fusion.17
  71.9 0.2 fusion.16
  72.1 0.2 fusion.15
  72.3 0.2 fusion.14
  72.5 0.2 fusion.13
  72.6 0.2 fusion.12
  74.0 3.4 copy-done.1
  77.4 4.5 copy.41
  82.0 2.5 dynamic_update_slice.12
  84.4 2.6 fusion.2
  87.0 2.8 fusion.1
  89.8 2.5 fusion
  92.3 6.2 %copy.44 = f32[17,128,512]{2,0,1:T(8,128)} copy(f32[17,128,512]{1,2,0:T(8,128)} %fusion) | data formatting | bytes 8912896 | tf_op jit(solution)/shard_map/dynamic_update_slice | solution.py:51
  98.6 380.4 %reduce-scatter.2.cloned.1.call-done = f32[17,2,512]{2,0,1:T(8,128)} async-done(((f32[17,128,512]{2,0,1:T(8,128)}), f32[17,2,512]{2,0,1:T(8,128)}) %reduce-scatter.2.cloned.1.call-update) | async-done | bytes 69648 | tf_op jit(solution)/shard_map/reduce_scatter | solution.py:52
  479.0 1.6 copy.45
  (53 shorter events, 6.0 us)
Async XLA Ops:
  6.5 37.4 %all-gather.2.cloned.1.call-start = ((), (), s32[]{:S(2)}) async-start(), calls=%async_computation.1 | async-start | bytes 1474560 | tf_op jit(solution)/shard_map/all_gather | solution.py:43
  9.3 469.7 %reduce-scatter.2.cloned.1.call-start = ((), (), s32[]{:S(2)}) async-start(), calls=%async_computation.2 | async-start | bytes 6389760 | tf_op jit(solution)/shard_map/reduce_scatter | solution.py:52
  49.5 1.8 copy-start
  73.9 10.6 %slice-start = ((s8[5013504]{0:T(1024)(128)(4,1)}), s8[4194304]{0:T(1024)(128)(4,1)S(1)}, s32[]{:S(2)}) async-start(s8[5013504]{0:T(1024)(128)(4,1)} %bitcast.330), calls=%async_computation.3 | async-start | bytes 8388608
  74.0 3.4 copy-start.1
  77.4 7.0 %slice-start.1 = ((s8[5013504]{0:T(1024)(128)(4,1)}), s8[819200]{0:T(1024)(128)(4,1)S(1)}, s32[]{:S(2)}) async-start(s8[5013504]{0:T(1024)(128)(4,1)} %bitcast.330), calls=%async_computation.4 | async-start | bytes 1638400
  77.4 9.6 %slice-start.2 = ((s8[5013504]{0:T(1024)(128)(4,1)}), s8[4194304]{0:T(1024)(128)(4,1)S(1)}, s32[]{:S(2)}) async-start(s8[5013504]{0:T(1024)(128)(4,1)} %bitcast.333), calls=%async_computation.5 | async-start | bytes 8388608
  81.9 5.1 %slice-start.3 = ((s8[5013504]{0:T(1024)(128)(4,1)}), s8[819200]{0:T(1024)(128)(4,1)S(1)}, s32[]{:S(2)}) async-start(s8[5013504]{0:T(1024)(128)(4,1)} %bitcast.333), calls=%async_computation.6 | async-start | bytes 1638400
Sparse Core Ops, SparseCore 0:
  9.4 34.5 all-gather.1
  98.7 380.2 reduce-scatter.1
where the time goes:
time: 488 us; the launch traced here: 487 us
  waiting for transfers between devices  414 us (85%)
  local copies, waits for them, and re-layouts  47.7 us (10%)
  between operations  13.6 us (3%)
  matrix products  9.43 us (2%)
    reduce_scatter x1, waiting for transfers between devices, on_device(): return lax.psum_scatter(totals, 'st', scatter_dimension=1, tiled=True)  380 us
    all_gather x1, waiting for transfers between devices, on_device(): gathered = lax.all_gather(unit_waves, 'ev', axis=1, tiled=True)  34 us
    unnamed x77, local copies, waits for them, and re-layouts  15.5 us
    transpose x4, local copies, waits for them, and re-layouts, lag_stack(): return shifted.reshape(LAGS, rows_other, 3 * samples)  13.4 us
  transfers between devices with their start and end apart: 2, of which 2 were waited for; matrix products, arithmetic and copies ran while one was open for 0% of the time, Pallas kernels for 0%

commit v1 on v0

v1 whole, which is shorter than its diff:
```python
import functools

import jax
import jax.numpy as jnp
from jax import lax
from jax.experimental import pallas as pl
from jax.experimental.pallas import tpu as pltpu
from jax.sharding import PartitionSpec as P

LAGS = 17
EPSILON = 1e-06
MESH = pl.DeviceIdType.MESH
GROUPS = ((0, 9), (9, 8))
CHUNKS = 4


def place():
    ev, st = lax.axis_index("ev"), lax.axis_index("st")
    return ev, st // 16, (st // 4) % 4, st % 4


def at(ev, x, z, y):
    return (ev, x * 16 + z * 4 + y)


def along(axis, step):
    ev, x, z, y = place()
    if axis == "x":
        return at(ev, (x + step) % 4, z, y)
    if axis == "y":
        return at(ev, x, z, (y + step) % 4)
    return at(ev, x, (z + step) % 4, y)


def kernel(
    offset_ref, wave_ref, avail_ref, out_ref,
    unit, lhs, own, send1, recv1, send2, recv2, send3, recv3,
    gs, gr, ss1, rs1, ss2, rs2, ss3, rs3,
):
    ev, x, z, y = place()
    sibling = at(ev ^ 1, x, z, y)
    partner = at(ev ^ 2, x, z, y)
    stations = wave_ref.shape[0]

    barrier = pltpu.get_barrier_semaphore()
    peers = [along(a, d) for a in "xyz" for d in (1, 2, 3)] + [sibling, partner]
    for peer in peers:
        pl.semaphore_signal(barrier, inc=1, device_id=peer, device_id_type=MESH)

    row = lax.broadcasted_iota(jnp.int32, (128, 128), 0)
    col = lax.broadcasted_iota(jnp.int32, (128, 128), 1)
    for s in range(stations):
        wave = wave_ref[s].astype(jnp.float32)
        energy = jnp.sum(wave * wave, axis=-1, keepdims=True)
        here = avail_ref[pl.ds(s, 1), :].astype(jnp.float32)
        avail = jnp.sum(jnp.where(row == col, here, 0.0), axis=-1, keepdims=True)
        scaled = wave * (avail * lax.rsqrt(energy + EPSILON))
        unit[0, :, s * 384 : (s + 1) * 384] = scaled.astype(jnp.bfloat16)

    a, b, zr = row // 32, (row // 8) % 4, row % 8
    zz, r = zr // 2, zr % 2
    orders = (a * 32 + zz * 8 + b * 2 + r, b * 32 + zz * 8 + a * 2 + r)
    for s in range(stations):
        wave = unit[0, :, s * 384 : (s + 1) * 384]
        for (first, count), order in zip(GROUPS, orders):
            pick = (order == col).astype(jnp.float32).astype(jnp.bfloat16)
            rows = jnp.dot(pick, wave, preferred_element_type=jnp.float32).astype(jnp.bfloat16)
            stack = jnp.concatenate([rows[:, c * 128 : (c + 1) * 128] for c in range(3)], axis=0)
            moves = jnp.concatenate(
                [
                    (col - row == first + k - 8 + offset_ref[s]).astype(jnp.float32).astype(jnp.bfloat16)
                    for k in range(count)
                ],
                axis=1,
            )
            moved = jnp.dot(stack, moves, preferred_element_type=jnp.float32).astype(jnp.bfloat16)
            for k in range(count):
                for c in range(3):
                    lhs[
                        (first + k) * 128 : (first + k + 1) * 128,
                        s * 384 + c * 128 : s * 384 + (c + 1) * 128,
                    ] = moved[c * 128 : (c + 1) * 128, k * 128 : (k + 1) * 128]

    def remote(src, dst, send_sem, recv_sem, target):
        return pltpu.make_async_remote_copy(
            src_ref=src, dst_ref=dst, send_sem=send_sem, recv_sem=recv_sem,
            device_id=target, device_id_type=MESH,
        )

    def multiply(chunk):
        for first, count in GROUPS:
            total = lax.dot_general(
                lhs[first * 128 : (first + count) * 128, :], unit[chunk],
                (((1,), (1,)), ((), ())), preferred_element_type=jnp.float32,
            ).reshape(count, 128, 128)
            own[chunk, first : first + count] = total
            send1[chunk, first : first + count] = total.astype(jnp.bfloat16)

    firsts, seconds = ("x", "y"), ("y", "x")
    index = {"x": x, "y": y, "z": z}

    def stage1(chunk):
        copies = []
        for g, (first, count) in enumerate(GROUPS):
            for d in (1, 2, 3):
                to = (index[firsts[g]] + d) % 4
                copies.append(remote(
                    send1.at[chunk, pl.ds(first, count), pl.ds(pl.multiple_of(to * 32, 32), 32)],
                    recv1.at[chunk, d - 1, pl.ds(first, count)],
                    ss1.at[chunk, g, d - 1], rs1.at[chunk, g, d - 1], along(firsts[g], d),
                ))
        for copy in copies:
            copy.start()
        return copies

    def stage2(chunk, before):
        copies = []
        for g, (first, count) in enumerate(GROUPS):
            for copy in before[3 * g : 3 * g + 3]:
                copy.wait_recv()
            mine = pl.ds(pl.multiple_of(index[firsts[g]] * 32, 32), 32)
            lags = pl.ds(first, count)
            total = own[chunk, lags, mine]
            for d in range(3):
                total = total + recv1[chunk, d, lags].astype(jnp.float32)
            send2[chunk, lags] = total
            for d in (1, 2, 3):
                to = (index[seconds[g]] + d) % 4
                copy = remote(
                    send2.at[chunk, lags, pl.ds(pl.multiple_of(to * 8, 8), 8)],
                    recv2.at[chunk, d - 1, lags],
                    ss2.at[chunk, g, d - 1], rs2.at[chunk, g, d - 1], along(seconds[g], d),
                )
                copy.start()
                copies.append(copy)
        return copies

    def stage3(chunk, before):
        for g, (first, count) in enumerate(GROUPS):
            for copy in before[3 * g : 3 * g + 3]:
                copy.wait_recv()
            mine = pl.ds(pl.multiple_of(index[seconds[g]] * 8, 8), 8)
            lags = pl.ds(first, count)
            total = send2[chunk, lags, mine]
            for d in range(3):
                total = total + recv2[chunk, d, lags]
            for k in range(count):
                for to in range(4):
                    send3[chunk, to, 2 * (first + k) : 2 * (first + k) + 2] = total[k, 2 * to : 2 * to + 2]
        copies = []
        for d in (1, 2, 3):
            copy = remote(
                send3.at[chunk, (z + d) % 4], recv3.at[chunk, d - 1],
                ss3.at[chunk, d - 1], rs3.at[chunk, d - 1], along("z", d),
            )
            copy.start()
            copies.append(copy)
        return copies

    def finish(chunk, before):
        for copy in before:
            copy.wait_recv()
        total = send3[chunk, z]
        for d in range(3):
            total = total + recv3[chunk, d]
        return total

    multiply(0)
    pl.semaphore_wait(barrier, len(peers))

    gather = [
        remote(
            unit.at[0, pl.ds(64 * h, 64)], unit.at[2 + h, pl.ds(0, 64)], gs.at[h], gr.at[h], partner
        )
        for h in range(2)
    ]
    across = remote(unit.at[0], unit.at[1], gs.at[2], gr.at[2], sibling)
    relay = [
        remote(
            unit.at[2 + h, pl.ds(0, 64)], unit.at[2 + h, pl.ds(64, 64)], gs.at[3 + h], gr.at[3 + h], sibling
        )
        for h in range(2)
    ]
    gather[0].start()
    gather[1].start()
    across.start()
    first = [stage1(0)]
    across.wait_recv()
    multiply(1)
    first.append(stage1(1))
    second = [stage2(0, first[0])]
    second.append(stage2(1, first[1]))
    gather[0].wait_recv()
    relay[0].start()
    third = [stage3(0, second[0])]
    relay[0].wait_recv()
    multiply(2)
    first.append(stage1(2))
    third.append(stage3(1, second[1]))
    gather[1].wait_recv()
    relay[1].start()
    second.append(stage2(2, first[2]))
    relay[1].wait_recv()
    multiply(3)
    first.append(stage1(3))
    third.append(stage3(2, second[2]))
    for chunk in range(2):
        block = pl.ds(pl.multiple_of((ev ^ chunk) * 128, 128), 128)
        out_ref[:, block] = finish(chunk, third[chunk])
    second.append(stage2(3, first[3]))
    low = finish(2, third[2])
    third.append(stage3(3, second[3]))
    high = finish(3, third[3])
    left = lax.broadcasted_iota(jnp.int32, low.shape, 1) < 64
    near = pl.ds(pl.multiple_of((ev ^ 2) * 128, 128), 128)
    far = pl.ds(pl.multiple_of((ev ^ 3) * 128, 128), 128)
    out_ref[:, near] = jnp.where(left, low, pltpu.roll(high, 64, 1))
    out_ref[:, far] = jnp.where(left, pltpu.roll(low, 64, 1), high)

    for copy in [*gather, across, *relay]:
        copy.wait_send()
    for group in (first, second, third):
        for copies in group:
            for copy in copies:
                copy.wait_send()


def on_device(waveforms, availability, lag_offset):
    f32, bf16, dma = jnp.float32, jnp.bfloat16, pltpu.SemaphoreType.DMA
    stations, _, width = waveforms.shape
    depth = stations * width
    total = pl.pallas_call(
        kernel,
        out_shape=jax.ShapeDtypeStruct((2 * LAGS, 512), f32),
        in_specs=[
            pl.BlockSpec(memory_space=pltpu.SMEM),
            pl.BlockSpec(memory_space=pltpu.VMEM),
            pl.BlockSpec(memory_space=pltpu.VMEM),
        ],
        out_specs=pl.BlockSpec(memory_space=pltpu.VMEM),
        scratch_shapes=[
            pltpu.VMEM((CHUNKS, 128, depth), bf16),
            pltpu.VMEM((LAGS * 128, depth), bf16),
            pltpu.VMEM((CHUNKS, LAGS, 128, 128), f32),
            pltpu.VMEM((CHUNKS, LAGS, 128, 128), bf16),
            pltpu.VMEM((CHUNKS, 3, LAGS, 32, 128), bf16),
            pltpu.VMEM((CHUNKS, LAGS, 32, 128), f32),
            pltpu.VMEM((CHUNKS, 3, LAGS, 8, 128), f32),
            pltpu.VMEM((CHUNKS, 4, 2 * LAGS, 128), f32),
            pltpu.VMEM((CHUNKS, 3, 2 * LAGS, 128), f32),
            dma((5,)), dma((5,)),
            dma((CHUNKS, 2, 3)), dma((CHUNKS, 2, 3)),
            dma((CHUNKS, 2, 3)), dma((CHUNKS, 2, 3)),
            dma((CHUNKS, 3)), dma((CHUNKS, 3)),
        ],
        compiler_params=pltpu.CompilerParams(
            collective_id=0, has_side_effects=True, vmem_limit_bytes=48 << 20
        ),
    )(lag_offset, waveforms, availability)
    return total.reshape(LAGS, 2, 512)


def solution(mesh):
    placed = (P("st", "ev", None), P("st", "ev"), P("st"))
    return jax.shard_map(
        on_device,
        mesh=mesh,
        in_specs=placed,
        out_specs=P(None, ("ev", "st"), None),
        check_vma=False,
    )
```

time: 488 us -> 48.6 us (0.10)
  the two profiles are of different devices: /device:TPU:0 before, /device:TPU:1 now
where the time goes in v1:
time: 48.6 us; the launch traced here: 48.3 us
  Pallas kernels  45.3 us (93%)
  local copies, waits for them, and re-layouts  2.97 us (6%)
    pallas_call x1, Pallas kernels, on_device(): pl.pallas_call(kernel, out_shape=jax.ShapeDtypeStruct((2 * LAGS, 512), f3...  45.3 us
    unnamed x6, local copies, waits for them, and re-layouts  2.3 us

profile of v1, /device:TPU:1, one launch (start us, length us, event | category | flops | bytes accessed | tf_op | source)
XLA Modules:
  0.0 48.3 jit_solution(4843115205479675707)
XLA Ops:
  0.0 0.0 copy-start
  0.0 1.0 %copy-done = bf16[3,128,384]{2,1,0:T(8,128)(2,1)S(1)} copy-done((bf16[3,128,384]{2,1,0:T(8,128)(2,1)S(1)}, bf16[3,128,384]{2,1,0:T(8,128)(2,1)}, u32[]{:S(2)}) %copy-start) | copy-done | bytes 294936
  1.0 0.0 copy-start.1
  1.0 0.7 %copy-done.1 = s32[3,128]{1,0:T(4,128)S(1)} copy-done((s32[3,128]{1,0:T(4,128)S(1)}, s32[3,128]{1,0:T(4,128)}, u32[]{:S(2)}) %copy-start.1) | copy-done | bytes 1560
  1.6 0.0 copy-start.2
  1.6 0.7 %copy-done.2 = s32[3]{0:T(128)S(1)} copy-done((s32[3]{0:T(128)S(1)}, s32[3]{0:T(128)}, u32[]{:S(2)}) %copy-start.2) | copy-done | bytes 36
  2.3 45.3 %shard_map.37 = f32[34,512]{1,0:T(8,128)S(1)} custom-call(s32[3]{0:T(128)S(1)} %copy-done.2, bf16[3,128,384]{2,1,0:T(8,128)(2,1)S(1)} %copy-done, s32[3,128]{1,0:T(4,128)S(1)} %copy-done.1), custom_call_target="tpu_custom_call" | custom-call | tf_op jit(solution)/shard_map/pallas_call | solution.py:232
  47.6 0.7 %reshape.3 = f32[17,2,512]{2,1,0:T(2,128)} reshape(f32[34,512]{1,0:T(8,128)S(1)} %shard_map.37) | data formatting | bytes 139264 | tf_op jit(solution)/shard_map/reshape | solution.py:260
Async XLA Ops:
  0.0 1.0 %copy-start = (bf16[3,128,384]{2,1,0:T(8,128)(2,1)S(1)}, bf16[3,128,384]{2,1,0:T(8,128)(2,1)}, u32[]{:S(2)}) copy-start(bf16[3,128,384]{2,1,0:T(8,128)(2,1)} %wave_ref.1) | copy-start | bytes 884740
  1.0 0.7 %copy-start.1 = (s32[3,128]{1,0:T(4,128)S(1)}, s32[3,128]{1,0:T(4,128)}, u32[]{:S(2)}) copy-start(s32[3,128]{1,0:T(4,128)} %avail_ref.1) | copy-start | bytes 4612
  1.6 0.7 %copy-start.2 = (s32[3]{0:T(128)S(1)}, s32[3]{0:T(128)}, u32[]{:S(2)}) copy-start(s32[3]{0:T(128)} %offset_ref.1) | copy-start | bytes 40

commit v2 on v0

v2 whole, which is shorter than its diff:
```python
import jax
import jax.numpy as jnp
from jax import lax
from jax.experimental import pallas as pl
from jax.experimental.pallas import tpu as pltpu
from jax.sharding import PartitionSpec as P

LAGS = 17
EPSILON = 1e-06
MESH = pl.DeviceIdType.MESH
ORDERS = ((0, 2, 4, 6, 8, 1, 3, 5, 7), (9, 11, 13, 15, 10, 12, 14, 16))
STARTS = (0, 9)
FIRSTS, SECONDS = ("x", "y"), ("y", "x")
CHUNKS = ((0, 128), (128, 128), (256, 128), (384, 64), (448, 64))


def tiles(chunk, group):
    counts = [
        [len(o) if rows == 128 else (len(o) + 1) // 2 for o in ORDERS] for _, rows in CHUNKS
    ]
    first = sum(sum(c) for c in counts[:chunk]) + sum(counts[chunk][:group])
    return first, counts[chunk][group]


def pairs(chunk, group):
    first = sum((tiles(c, g)[1] + 1) // 2 for c in range(chunk) for g in range(2))
    first += sum((tiles(chunk, g)[1] + 1) // 2 for g in range(group))
    return first, (tiles(chunk, group)[1] + 1) // 2


TILES = sum(tiles(c, g)[1] for c in range(len(CHUNKS)) for g in range(2))
PAIRS = sum(pairs(c, g)[1] for c in range(len(CHUNKS)) for g in range(2))


def place():
    ev, st = lax.axis_index("ev"), lax.axis_index("st")
    return ev, st // 16, (st // 4) % 4, st % 4


def at(ev, x, z, y):
    return (ev, x * 16 + z * 4 + y)


def along(axis, step):
    ev, x, z, y = place()
    if axis == "x":
        return at(ev, (x + step) % 4, z, y)
    if axis == "y":
        return at(ev, x, z, (y + step) % 4)
    return at(ev, x, (z + step) % 4, y)


def ones_where(mask):
    return mask.astype(jnp.float32).astype(jnp.bfloat16)


def kernel(
    offset_hbm, wave_hbm, avail_hbm, out_ref,
    offset_ref, wave_ref, avail_ref, unit, lhs, own, send1, recv1, own2, send2, recv2, wide3, wide_in, thin3, thin_in,
    ins, gs, gr, ss1, rs1, ss2, rs2, ss3, rs3,
):
    ev, x, z, y = place()
    index = {"x": x, "y": y, "z": z}
    sibling = at(ev ^ 1, x, z, y)
    partner = at(ev ^ 2, x, z, y)
    stations = wave_ref.shape[0]

    barrier = pltpu.get_barrier_semaphore()
    peers = [along(a, d) for a in "xyz" for d in (1, 2, 3)] + [sibling, partner]
    for peer in peers:
        pl.semaphore_signal(barrier, inc=1, device_id=peer, device_id_type=MESH)

    loads = [
        pltpu.make_async_copy(wave_hbm, wave_ref, ins.at[0]),
        pltpu.make_async_copy(avail_hbm, avail_ref, ins.at[1]),
        pltpu.make_async_copy(offset_hbm, offset_ref, ins.at[2]),
    ]
    for load in loads:
        load.start()
    for load in loads:
        load.wait()

    row = lax.broadcasted_iota(jnp.int32, (128, 128), 0)
    col = lax.broadcasted_iota(jnp.int32, (128, 128), 1)
    for s in range(stations):
        wave = wave_ref[s].astype(jnp.float32)
        energy = jnp.sum(wave * wave, axis=-1, keepdims=True)
        here = avail_ref[pl.ds(s, 1), :].astype(jnp.float32)
        avail = jnp.sum(jnp.where(row == col, here, 0.0), axis=-1, keepdims=True)
        scaled = wave * (avail * lax.rsqrt(energy + EPSILON))
        unit[0:128, s * 384 : (s + 1) * 384] = scaled.astype(jnp.bfloat16)

    def remote(src, dst, send_sem, recv_sem, target):
        return pltpu.make_async_remote_copy(
            src_ref=src, dst_ref=dst, send_sem=send_sem, recv_sem=recv_sem,
            device_id=target, device_id_type=MESH,
        )

    pl.semaphore_wait(barrier, len(peers))

    parts = ((0, 64, 256), (64, 32, 384), (96, 32, 448))
    gather = [
        remote(unit.at[pl.ds(low, n)], unit.at[pl.ds(to, n)], gs.at[h], gr.at[h], partner)
        for h, (low, n, to) in enumerate(parts)
    ]
    across = remote(unit.at[pl.ds(0, 128)], unit.at[pl.ds(128, 128)], gs.at[3], gr.at[3], sibling)
    relay = [
        remote(unit.at[pl.ds(to, n)], unit.at[pl.ds(to + n, n)], gs.at[4 + h], gr.at[4 + h], sibling)
        for h, (_, n, to) in enumerate(parts)
    ]

    for copy in gather:
        copy.start()
    across.start()

    a, b, zr = row // 32, (row // 8) % 4, row % 8
    zz, r = zr // 2, zr % 2
    places = (a * 32 + zz * 8 + b * 2 + r, b * 32 + zz * 8 + a * 2 + r)
    for s in range(stations):
        wave = unit[0:128, s * 384 : (s + 1) * 384]
        for start, order, source in zip(STARTS, ORDERS, places):
            rows = jnp.dot(ones_where(source == col), wave, preferred_element_type=jnp.float32).astype(jnp.bfloat16)
            stack = jnp.concatenate([rows[:, c * 128 : (c + 1) * 128] for c in range(3)], axis=0)
            moves = jnp.concatenate([ones_where(col - row == lag - 8 + offset_ref[s]) for lag in order], axis=1)
            moved = jnp.dot(stack, moves, preferred_element_type=jnp.float32).astype(jnp.bfloat16)
            for k in range(len(order)):
                for c in range(3):
                    lhs[
                        (start + k) * 128 : (start + k + 1) * 128,
                        s * 384 + c * 128 : s * 384 + (c + 1) * 128,
                    ] = moved[c * 128 : (c + 1) * 128, k * 128 : (k + 1) * 128]

    def multiply(chunk, group):
        at_row, rows = CHUNKS[chunk]
        first, count = tiles(chunk, group)
        start, order = STARTS[group], ORDERS[group]

        def dot(low, high):
            return lax.dot_general(
                lhs[(start + low) * 128 : (start + high) * 128, :], unit[at_row : at_row + rows, :],
                (((1,), (1,)), ((), ())), preferred_element_type=jnp.float32,
            )

        if rows == 128:
            total = dot(0, count)
        else:
            left, right = dot(0, count), dot(count, len(order))
            if len(order) % 2:
                right = jnp.concatenate([right, jnp.zeros((128, rows), jnp.float32)], axis=0)
            total = jnp.concatenate([left, right], axis=1)
        total = total.reshape(count, 128, 128)
        own[first : first + count] = total
        send1[first : first + count] = total.astype(jnp.bfloat16)

    def copies1(chunk, group):
        first, count = tiles(chunk, group)
        some = pl.ds(first, count)
        axis = FIRSTS[group]
        return [
            remote(
                send1.at[some, pl.ds(pl.multiple_of((index[axis] + d) % 4 * 32, 32), 32)],
                recv1.at[d - 1, some],
                ss1.at[chunk, group, d - 1], rs1.at[chunk, group, d - 1], along(axis, d),
            )
            for d in (2, 1, 3)
        ]

    def stage1(chunk):
        copies = [None, None]
        for group in range(2):
            multiply(chunk, group)
            copies[group] = copies1(chunk, group)
            for copy in copies[group]:
                copy.start()
        return copies

    def stage2(chunk, before):
        copies = [None, None]
        for group in range(2):
            for copy in before[group]:
                copy.wait_recv()
            first, count = tiles(chunk, group)
            pair, half = pairs(chunk, group)
            total = own[first : first + count, pl.ds(pl.multiple_of(index[FIRSTS[group]] * 32, 32), 32)]
            for d in range(3):
                total = total + recv1[d, first : first + count].astype(jnp.float32)
            own2[first : first + count] = total
            for p in range(half):
                one, two = total[2 * p], total[min(2 * p + 1, count - 1)]
                for to in range(4):
                    both = jnp.concatenate([one[8 * to : 8 * to + 8], two[8 * to : 8 * to + 8]], axis=0)
                    send2[to, pair + p] = both.astype(jnp.bfloat16)
            axis = SECONDS[group]
            copies[group] = [
                remote(
                    send2.at[(index[axis] + d) % 4, pl.ds(pair, half)], recv2.at[d - 1, pl.ds(pair, half)],
                    ss2.at[chunk, group, d - 1], rs2.at[chunk, group, d - 1], along(axis, d),
                )
                for d in (2, 1, 3)
            ]
            for copy in copies[group]:
                copy.start()
        return copies

    def buffers3(chunk):
        return (wide3.at[chunk], wide_in.at[chunk]) if chunk < 3 else (thin3.at[chunk - 3], thin_in.at[chunk - 3])

    def stage3(chunk, before):
        out3, in3 = buffers3(chunk)
        base = tiles(chunk, 0)[0]
        for group in range(2):
            for copy in before[group]:
                copy.wait_recv()
            first, count = tiles(chunk, group)
            pair, half = pairs(chunk, group)
            mine = own2[first : first + count, pl.ds(pl.multiple_of(index[SECONDS[group]] * 8, 8), 8)]
            others = recv2[0, pair : pair + half].astype(jnp.float32)
            for d in (1, 2):
                others = others + recv2[d, pair : pair + half].astype(jnp.float32)
            for k in range(count):
                total = mine[k] + others[k // 2, k % 2 * 8 : k % 2 * 8 + 8]
                place3 = 2 * (ORDERS[group][k] if chunk < 3 else first + k - base)
                for to in range(4):
                    out3[to, place3 : place3 + 2] = total[2 * to : 2 * to + 2]
        copies = [
            remote(
                out3.at[(z + d) % 4], in3.at[d - 1],
                ss3.at[chunk, d - 1], rs3.at[chunk, d - 1], along("z", d),
            )
            for d in (2, 1, 3)
        ]
        for copy in copies:
            copy.start()
        return copies

    def finish(chunk, before):
        out3, in3 = buffers3(chunk)
        for copy in before:
            copy.wait_recv()
        total = out3[z]
        for d in range(3):
            total = total + in3[d]
        if chunk < 3:
            return total
        halves = (total, pltpu.roll(total, 64, 1))
        rows = []
        for lag in range(LAGS):
            group = 0 if lag in ORDERS[0] else 1
            first, count = tiles(chunk, group)
            k = ORDERS[group].index(lag)
            at_row = 2 * (first - tiles(chunk, 0)[0] + k % count)
            rows.append(halves[k // count][at_row : at_row + 2])
        return jnp.concatenate(rows, axis=0)

    def pass_on(h):
        gather[h].wait_recv()
        relay[h].start()

    first, second, third = {}, {}, {}
    first[0] = stage1(0)
    across.wait_recv()
    first[1] = stage1(1)
    second[0] = stage2(0, first[0])
    pass_on(0)
    relay[0].wait_recv()
    first[2] = stage1(2)
    second[1] = stage2(1, first[1])
    pass_on(1)
    relay[1].wait_recv()
    first[3] = stage1(3)
    pass_on(2)
    relay[2].wait_recv()
    first[4] = stage1(4)
    for chunk in (0, 1):
        third[chunk] = stage3(chunk, second[chunk])
    for chunk in (2, 3, 4):
        second[chunk] = stage2(chunk, first[chunk])
    for chunk in (2, 3, 4):
        third[chunk] = stage3(chunk, second[chunk])
    for chunk in range(2):
        block = pl.ds(pl.multiple_of((ev ^ chunk) * 128, 128), 128)
        out_ref[:, block] = finish(chunk, third[chunk])
    half, quarter, last = (finish(chunk, third[chunk]) for chunk in (2, 3, 4))
    lane = lax.broadcasted_iota(jnp.int32, half.shape, 1)
    near = pl.ds(pl.multiple_of((ev ^ 2) * 128, 128), 128)
    far = pl.ds(pl.multiple_of((ev ^ 3) * 128, 128), 128)
    out_ref[:, near] = jnp.where(
        lane < 64, half, jnp.where(lane < 96, pltpu.roll(quarter, 64, 1), pltpu.roll(last, 96, 1))
    )
    out_ref[:, far] = jnp.where(
        lane < 64, pltpu.roll(half, 64, 1),
        jnp.where(lane < 96, pltpu.roll(quarter, 32, 1), pltpu.roll(last, 64, 1)),
    )

    for copy in [*gather, across, *relay]:
        copy.wait_send()
    for chunk in range(len(CHUNKS)):
        for copy in [*first[chunk][0], *first[chunk][1], *second[chunk][0], *second[chunk][1], *third[chunk]]:
            copy.wait_send()


def on_device(waveforms, availability, lag_offset):
    f32, bf16, dma = jnp.float32, jnp.bfloat16, pltpu.SemaphoreType.DMA
    stations, _, width = waveforms.shape
    depth = stations * width
    chunks = len(CHUNKS)
    total = pl.pallas_call(
        kernel,
        out_shape=pltpu.VMEM((2 * LAGS, 512), f32),
        in_specs=[pl.BlockSpec(memory_space=pltpu.HBM)] * 3,
        out_specs=pl.BlockSpec(memory_space=pltpu.VMEM),
        scratch_shapes=[
            pltpu.SMEM(lag_offset.shape, jnp.int32),
            pltpu.VMEM(waveforms.shape, bf16),
            pltpu.VMEM(availability.shape, jnp.int32),
            pltpu.VMEM((512, depth), bf16),
            pltpu.VMEM((LAGS * 128, depth), bf16),
            pltpu.VMEM((TILES, 128, 128), f32),
            pltpu.VMEM((TILES, 128, 128), bf16),
            pltpu.VMEM((3, TILES, 32, 128), bf16),
            pltpu.VMEM((TILES, 32, 128), f32),
            pltpu.VMEM((4, PAIRS, 16, 128), bf16),
            pltpu.VMEM((3, PAIRS, 16, 128), bf16),
            pltpu.VMEM((3, 4, 2 * LAGS, 128), f32),
            pltpu.VMEM((3, 3, 2 * LAGS, 128), f32),
            pltpu.VMEM((2, 4, LAGS + 1, 128), f32),
            pltpu.VMEM((2, 3, LAGS + 1, 128), f32),
            dma((3,)),
            dma((7,)), dma((7,)),
            dma((chunks, 2, 3)), dma((chunks, 2, 3)),
            dma((chunks, 2, 3)), dma((chunks, 2, 3)),
            dma((chunks, 3)), dma((chunks, 3)),
        ],
        compiler_params=pltpu.CompilerParams(
            collective_id=0, has_side_effects=True, vmem_limit_bytes=60 << 20
        ),
    )(lag_offset, waveforms, availability)
    return total.reshape(LAGS, 2, 512)


def solution(mesh):
    placed = (P("st", "ev", None), P("st", "ev"), P("st"))
    return jax.shard_map(
        on_device,
        mesh=mesh,
        in_specs=placed,
        out_specs=P(None, ("ev", "st"), None),
        check_vma=False,
    )
```

time: 488 us -> 43.8 us (0.09)
  the two profiles are of different devices: /device:TPU:0 before, /device:TPU:1 now
where the time goes in v2:
time: 43.8 us; the launch traced here: 43.7 us
  Pallas kernels  43 us (98%)
  local copies, waits for them, and re-layouts  0.67 us (2%)
    pallas_call x1, Pallas kernels, on_device(): pl.pallas_call(kernel, out_shape=pltpu.VMEM((2 * LAGS, 512), f32), in_spe...  43 us

profile of v2, /device:TPU:1, one launch (start us, length us, event | category | flops | bytes accessed | tf_op | source)
XLA Modules:
  0.0 43.7 jit_solution(2519928521050951663)
XLA Ops:
  0.0 43.0 %shard_map.37 = f32[34,512]{1,0:T(8,128)S(1)} custom-call(s32[3]{0:T(128)} %offset_hbm.1, bf16[3,128,384]{2,1,0:T(8,128)(2,1)} %wave_hbm.1, s32[3,128]{1,0:T(4,128)} %avail_hbm.1), custom_call_target="tpu_custom_call" | custom-call | tf_op jit(solution)/shard_map/pallas_call | solution.py:307
  43.0 0.7 %reshape.3 = f32[17,2,512]{2,1,0:T(2,128)} reshape(f32[34,512]{1,0:T(8,128)S(1)} %shard_map.37) | data formatting | bytes 139264 | tf_op jit(solution)/shard_map/reshape | solution.py:338

commit v3 on v2

--- a/solution.py
+++ b/solution.py
@@ -8,15 +8,20 @@
 LAGS = 17
 EPSILON = 1e-06
 MESH = pl.DeviceIdType.MESH
-ORDERS = ((0, 2, 4, 6, 8, 1, 3, 5, 7), (9, 11, 13, 15, 10, 12, 14, 16))
-STARTS = (0, 9)
+ORDERS = ((8, 0, 2, 4, 6, 1, 3, 5, 7), (8, 9, 11, 13, 15, 10, 12, 14, 16))
+DEPTH = len(ORDERS[0])
 FIRSTS, SECONDS = ("x", "y"), ("y", "x")
 CHUNKS = ((0, 128), (128, 128), (256, 128), (384, 64), (448, 64))
 
 
+def lags(chunk, group):
+    return ORDERS[group][(chunk + group) % 2 :]
+
+
 def tiles(chunk, group):
     counts = [
-        [len(o) if rows == 128 else (len(o) + 1) // 2 for o in ORDERS] for _, rows in CHUNKS
+        [len(lags(c, g)) if rows == 128 else (len(lags(c, g)) + 1) // 2 for g in range(2)]
+        for c, (_, rows) in enumerate(CHUNKS)
     ]
     first = sum(sum(c) for c in counts[:chunk]) + sum(counts[chunk][:group])
     return first, counts[chunk][group]
@@ -109,16 +114,17 @@
         for h, (_, n, to) in enumerate(parts)
     ]
 
-    for copy in gather:
-        copy.start()
+    gather[0].start()
     across.start()
 
     a, b, zr = row // 32, (row // 8) % 4, row % 8
     zz, r = zr // 2, zr % 2
     places = (a * 32 + zz * 8 + b * 2 + r, b * 32 + zz * 8 + a * 2 + r)
-    for s in range(stations):
-        wave = unit[0:128, s * 384 : (s + 1) * 384]
-        for start, order, source in zip(STARTS, ORDERS, places):
+
+    def shift_rows(group):
+        order, source, start = ORDERS[group], places[group], DEPTH * group
+        for s in range(stations):
+            wave = unit[0:128, s * 384 : (s + 1) * 384]
             rows = jnp.dot(ones_where(source == col), wave, preferred_element_type=jnp.float32).astype(jnp.bfloat16)
             stack = jnp.concatenate([rows[:, c * 128 : (c + 1) * 128] for c in range(3)], axis=0)
             moves = jnp.concatenate([ones_where(col - row == lag - 8 + offset_ref[s]) for lag in order], axis=1)
@@ -133,7 +139,8 @@
     def multiply(chunk, group):
         at_row, rows = CHUNKS[chunk]
         first, count = tiles(chunk, group)
-        start, order = STARTS[group], ORDERS[group]
+        order = lags(chunk, group)
+        start = DEPTH * (group + 1) - len(order)
 
         def dot(low, high):
             return lax.dot_general(
@@ -151,6 +158,17 @@
         total = total.reshape(count, 128, 128)
         own[first : first + count] = total
         send1[first : first + count] = total.astype(jnp.bfloat16)
+
+    def multiply_own(group):
+        total = lax.dot_general(
+            lhs[DEPTH * group * 128 : DEPTH * (group + 1) * 128, :], unit[0:256, :],
+            (((1,), (1,)), ((), ())), preferred_element_type=jnp.float32,
+        )
+        for chunk in range(2):
+            first, count = tiles(chunk, group)
+            some = total[(DEPTH - count) * 128 :, chunk * 128 : (chunk + 1) * 128].reshape(count, 128, 128)
+            own[first : first + count] = some
+            send1[first : first + count] = some.astype(jnp.bfloat16)
 
     def copies1(chunk, group):
         first, count = tiles(chunk, group)
@@ -219,7 +237,7 @@
                 others = others + recv2[d, pair : pair + half].astype(jnp.float32)
             for k in range(count):
                 total = mine[k] + others[k // 2, k % 2 * 8 : k % 2 * 8 + 8]
-                place3 = 2 * (ORDERS[group][k] if chunk < 3 else first + k - base)
+                place3 = 2 * (lags(chunk, group)[k] if chunk < 3 else first + k - base)
                 for to in range(4):
                     out3[to, place3 : place3 + 2] = total[2 * to : 2 * to + 2]
         copies = [
@@ -245,9 +263,9 @@
         halves = (total, pltpu.roll(total, 64, 1))
         rows = []
         for lag in range(LAGS):
-            group = 0 if lag in ORDERS[0] else 1
+            group = 0 if lag in lags(chunk, 0) else 1
             first, count = tiles(chunk, group)
-            k = ORDERS[group].index(lag)
+            k = lags(chunk, group).index(lag)
             at_row = 2 * (first - tiles(chunk, 0)[0] + k % count)
             rows.append(halves[k // count][at_row : at_row + 2])
         return jnp.concatenate(rows, axis=0)
@@ -257,26 +275,39 @@
         relay[h].start()
 
     first, second, third = {}, {}, {}
-    first[0] = stage1(0)
-    across.wait_recv()
-    first[1] = stage1(1)
-    second[0] = stage2(0, first[0])
+    first[0], first[1] = [None, None], [None, None]
+    for group in range(2):
+        shift_rows(group)
+        if group == 0:
+            across.wait_recv()
+        multiply_own(group)
+        for chunk in range(2):
+            first[chunk][group] = copies1(chunk, group)
+            for copy in first[chunk][group]:
+                copy.start()
+    gather[0].wait_send()
+    gather[1].start()
     pass_on(0)
+    gather[1].wait_send()
+    gather[2].start()
     relay[0].wait_recv()
     first[2] = stage1(2)
-    second[1] = stage2(1, first[1])
+    second[0] = stage2(0, first[0])
     pass_on(1)
     relay[1].wait_recv()
     first[3] = stage1(3)
+    second[1] = stage2(1, first[1])
     pass_on(2)
     relay[2].wait_recv()
     first[4] = stage1(4)
-    for chunk in (0, 1):
-        third[chunk] = stage3(chunk, second[chunk])
-    for chunk in (2, 3, 4):
-        second[chunk] = stage2(chunk, first[chunk])
-    for chunk in (2, 3, 4):
-        third[chunk] = stage3(chunk, second[chunk])
+    second[2] = stage2(2, first[2])
+    second[3] = stage2(3, first[3])
+    third[0] = stage3(0, second[0])
+    third[1] = stage3(1, second[1])
+    second[4] = stage2(4, first[4])
+    third[2] = stage3(2, second[2])
+    third[3] = stage3(3, second[3])
+    third[4] = stage3(4, second[4])
     for chunk in range(2):
         block = pl.ds(pl.multiple_of((ev ^ chunk) * 128, 128), 128)
         out_ref[:, block] = finish(chunk, third[chunk])
@@ -292,7 +323,7 @@
         jnp.where(lane < 96, pltpu.roll(quarter, 32, 1), pltpu.roll(last, 64, 1)),
     )
 
-    for copy in [*gather, across, *relay]:
+    for copy in [gather[2], across, *relay]:
         copy.wait_send()
     for chunk in range(len(CHUNKS)):
         for copy in [*first[chunk][0], *first[chunk][1], *second[chunk][0], *second[chunk][1], *third[chunk]]:
@@ -314,7 +345,7 @@
             pltpu.VMEM(waveforms.shape, bf16),
             pltpu.VMEM(availability.shape, jnp.int32),
             pltpu.VMEM((512, depth), bf16),
-            pltpu.VMEM((LAGS * 128, depth), bf16),
+            pltpu.VMEM((2 * DEPTH * 128, depth), bf16),
             pltpu.VMEM((TILES, 128, 128), f32),
             pltpu.VMEM((TILES, 128, 128), bf16),
             pltpu.VMEM((3, TILES, 32, 128), bf16),

time: 43.8 us -> 41.8 us (0.954)
  Pallas kernels: 43 us -> 40.7 us
    pallas_call x1, Pallas kernels: 43 us -> 40.7 us  [on_device(): pl.pallas_call(kernel, out_shape=pltpu.VMEM((2 * LAGS, 512), f32), in_spe...]
where the time goes in v3:
time: 41.8 us; the launch traced here: 41.3 us
  Pallas kernels  40.7 us (97%)
  local copies, waits for them, and re-layouts  0.67 us (2%)
    pallas_call x1, Pallas kernels, on_device(): pl.pallas_call(kernel, out_shape=pltpu.VMEM((2 * LAGS, 512), f32), in_spe...  40.7 us

profile of v3, /device:TPU:1, one launch (start us, length us, event | category | flops | bytes accessed | tf_op | source)
XLA Modules:
  0.0 41.3 jit_solution(6516657185401784558)
XLA Ops:
  0.0 40.7 %shard_map.37 = f32[34,512]{1,0:T(8,128)S(1)} custom-call(s32[3]{0:T(128)} %offset_hbm.1, bf16[3,128,384]{2,1,0:T(8,128)(2,1)} %wave_hbm.1, s32[3,128]{1,0:T(4,128)} %avail_hbm.1), custom_call_target="tpu_custom_call" | custom-call | tf_op jit(solution)/shard_map/pallas_call | solution.py:338
  40.7 0.7 %reshape.3 = f32[17,2,512]{2,1,0:T(2,128)} reshape(f32[34,512]{1,0:T(8,128)S(1)} %shard_map.37) | data formatting | bytes 139264 | tf_op jit(solution)/shard_map/reshape | solution.py:369

commit v4 on v3

--- a/solution.py
+++ b/solution.py
@@ -71,7 +71,7 @@
     stations = wave_ref.shape[0]
 
     barrier = pltpu.get_barrier_semaphore()
-    peers = [along(a, d) for a in "xyz" for d in (1, 2, 3)] + [sibling, partner]
+    peers = [partner] + [along(a, d) for a in "zxy" for d in (1, 2, 3)] + [sibling]
     for peer in peers:
         pl.semaphore_signal(barrier, inc=1, device_id=peer, device_id_type=MESH)
 
@@ -308,6 +308,14 @@
     third[2] = stage3(2, second[2])
     third[3] = stage3(3, second[3])
     third[4] = stage3(4, second[4])
+    for copy in [gather[2], across, *relay]:
+        copy.wait_send()
+    for chunk in range(len(CHUNKS)):
+        for copy in [*first[chunk][0], *first[chunk][1], *second[chunk][0], *second[chunk][1]]:
+            copy.wait_send()
+    for chunk in range(len(CHUNKS) - 1):
+        for copy in third[chunk]:
+            copy.wait_send()
     for chunk in range(2):
         block = pl.ds(pl.multiple_of((ev ^ chunk) * 128, 128), 128)
         out_ref[:, block] = finish(chunk, third[chunk])
@@ -323,11 +331,8 @@
         jnp.where(lane < 96, pltpu.roll(quarter, 32, 1), pltpu.roll(last, 64, 1)),
     )
 
-    for copy in [gather[2], across, *relay]:
+    for copy in third[len(CHUNKS) - 1]:
         copy.wait_send()
-    for chunk in range(len(CHUNKS)):
-        for copy in [*first[chunk][0], *first[chunk][1], *second[chunk][0], *second[chunk][1], *third[chunk]]:
-            copy.wait_send()
 
 
 def on_device(waveforms, availability, lag_offset):

time: 41.8 us -> 41.7 us (level)
  no operation moved by 1% of the time
where the time goes in v4:
time: 41.7 us; the launch traced here: 41.4 us
  Pallas kernels  40.8 us (98%)
  local copies, waits for them, and re-layouts  0.67 us (2%)
    pallas_call x1, Pallas kernels, on_device(): pl.pallas_call(kernel, out_shape=pltpu.VMEM((2 * LAGS, 512), f32), in_spe...  40.8 us

profile of v4, /device:TPU:1, one launch (start us, length us, event | category | flops | bytes accessed | tf_op | source)
XLA Modules:
  0.0 41.4 jit_solution(5463439814832946319)
XLA Ops:
  0.0 40.8 %shard_map.37 = f32[34,512]{1,0:T(8,128)S(1)} custom-call(s32[3]{0:T(128)} %offset_hbm.1, bf16[3,128,384]{2,1,0:T(8,128)(2,1)} %wave_hbm.1, s32[3,128]{1,0:T(4,128)} %avail_hbm.1), custom_call_target="tpu_custom_call" | custom-call | tf_op jit(solution)/shard_map/pallas_call | solution.py:343
  40.8 0.7 %reshape.3 = f32[17,2,512]{2,1,0:T(2,128)} reshape(f32[34,512]{1,0:T(8,128)S(1)} %shard_map.37) | data formatting | bytes 139264 | tf_op jit(solution)/shard_map/reshape | solution.py:374

commit v5 on v4

--- a/solution.py
+++ b/solution.py
@@ -292,12 +292,12 @@
     gather[2].start()
     relay[0].wait_recv()
     first[2] = stage1(2)
+    pass_on(1)
     second[0] = stage2(0, first[0])
-    pass_on(1)
     relay[1].wait_recv()
     first[3] = stage1(3)
+    pass_on(2)
     second[1] = stage2(1, first[1])
-    pass_on(2)
     relay[2].wait_recv()
     first[4] = stage1(4)
     second[2] = stage2(2, first[2])

time: 41.7 us -> 41.6 us (level)
  no operation moved by 1% of the time
where the time goes in v5:
time: 41.6 us; the launch traced here: 41.4 us
  Pallas kernels  40.7 us (98%)
  local copies, waits for them, and re-layouts  0.67 us (2%)
    pallas_call x1, Pallas kernels, on_device(): pl.pallas_call(kernel, out_shape=pltpu.VMEM((2 * LAGS, 512), f32), in_spe...  40.7 us

profile of v5, /device:TPU:1, one launch (start us, length us, event | category | flops | bytes accessed | tf_op | source)
XLA Modules:
  0.0 41.4 jit_solution(8239064627353079368)
XLA Ops:
  0.0 40.7 %shard_map.37 = f32[34,512]{1,0:T(8,128)S(1)} custom-call(s32[3]{0:T(128)} %offset_hbm.1, bf16[3,128,384]{2,1,0:T(8,128)(2,1)} %wave_hbm.1, s32[3,128]{1,0:T(4,128)} %avail_hbm.1), custom_call_target="tpu_custom_call" | custom-call | tf_op jit(solution)/shard_map/pallas_call | solution.py:343
  40.7 0.7 %reshape.3 = f32[17,2,512]{2,1,0:T(2,128)} reshape(f32[34,512]{1,0:T(8,128)S(1)} %shard_map.37) | data formatting | bytes 139264 | tf_op jit(solution)/shard_map/reshape | solution.py:374
